TPU v7x, 256 devices: a whole 4x4x8 slice. The times are simulated.
256 devices in a mesh: seq: 32 (over y, x, core), head: 4 (over z_lo), dp: 2 (over z_hi).
Axes of the slice: x: 4, y: 4, z: 8 (z_hi: 2, z_lo: 4; z = z_hi * 4 + z_lo), core: 2. Of those that a mesh axis runs over, the one named last changes fastest.
Arguments:
- tokens: bfloat16 [8192, 4096], P(('dp', 'seq'), 'head'), parts along dimension 0, may hold values from -60 to 60
- w_key: bfloat16 [4096, 4096], P('seq', 'head'), may hold values from -0.09375 to 0.09375
- w_value: bfloat16 [4096, 4096], P('seq', 'head'), may hold values from -0.09375 to 0.09375
- w_query: bfloat16 [4096, 4096], P('seq', 'head'), may hold values from -0.1875 to 0.1875
- slot_queries: bfloat16 [512, 4096], P('dp', 'head'), parts along dimension 0, may hold values from -100 to 100
- memory: bfloat16 [512, 4096], P('dp', 'head'), parts along dimension 0, may hold values from -6 to 6
- norm_gain: float32 [4096], P('head'), may hold values from 0.5 to 1.5
- doc_length: int32 [2], P('dp'), parts along dimension 0, may hold values from 1024 to 4096
Outputs:
- unpacked: bfloat16 [8192, 4096], P(('dp', 'seq'), 'head'), parts along dimension 0
- new_memory: bfloat16 [512, 4096], P('dp', 'head'), parts along dimension 0
There are 2 independent parts, one for each index of `dp`. A program takes and returns all parts, laid end to end along the dimension named above; an argument that names none is the same for every part. Nothing has to cross between parts.
All inputs are finite; a program needn't handle non-finite values.
Results may differ from a plain program's by a relative error of at most 0.003.
The roundings to bfloat16 on the way count: a program that leaves them out, or rounds other values in their place, can miss the bound.
Values may be sent and summed in bfloat16 or wider, within the bound.
A program may use at most 192 MiB of HBM per device.

v0:
```python
import math

import jax
import jax.numpy as jnp
from jax import lax
from jax.experimental import pallas as pl
from jax.experimental.pallas import tpu as pltpu
from jax.sharding import PartitionSpec as P

D = 4096
HEAD_DIM = 128
NEGATIVE = -1e30
EPSILON = 1e-05
SCALING = 1.0 / math.sqrt(HEAD_DIM)
MESH = pl.DeviceIdType.MESH
F32 = jnp.float32
BF16 = jnp.bfloat16
NT = (((1,), (1,)), ((), ()))


def merge(pieces):
    outs, stats = [], []
    for h in range(2):
        tops = [p[:, 256 + 2 * h : 257 + 2 * h] for p in pieces]
        sums = [p[:, 257 + 2 * h : 258 + 2 * h] for p in pieces]
        accs = [p[:, h * 128 : (h + 1) * 128] for p in pieces]
        top = tops[0]
        for t in tops[1:]:
            top = jnp.maximum(top, t)
        factors = [jnp.exp(t - top) for t in tops]
        total = sum(s * f for s, f in zip(sums, factors))
        acc = sum(a * f for a, f in zip(accs, factors))
        outs.append(acc)
        stats.append((top, total))
    return outs, stats


def stat_lanes(stats, rows):
    lane = lax.broadcasted_iota(jnp.int32, (rows, 128), 1)
    (m0, s0), (m1, s1) = stats
    return jnp.where(lane == 0, m0, jnp.where(lane == 1, s0, jnp.where(lane == 2, m1, s1)))


def kernel(
    tok, wk, wv, wq, sq, mem, gain, dl,
    o_un, o_nm,
    tokb, wb, sqb, memb, gainb, dlb, acc, pm, pr, mg, mr, st, nmf, nx, ob,
    loc, z_s, z_r, zb_s, zb_r, xa_s, xa_r, f_s, f_r, xw_s, xw_r, yw_s, yw_r, cw_s, cw_r,
    p1, p2_s, p2_r, p3_s, p3_r, p4_s, p4_r, n_s, n_r, m_s, m_r, nc_s, nc_r, u_s, u_r,
):
    seq = lax.axis_index("seq")
    z = lax.axis_index("head")
    dp = lax.axis_index("dp")
    y, x, c = seq // 8, (seq // 2) % 4, seq % 2
    xs = [(x + d) % 4 for d in range(4)]
    ys = [(y + d) % 4 for d in range(4)]
    zs = [(z + d) % 4 for d in range(4)]

    def dev(x=x, y=y, z=z, c=c):
        return (y * 8 + x * 2 + c, z, dp)

    def remote(src, dst, send, recv, to):
        return pltpu.make_async_remote_copy(
            src_ref=src, dst_ref=dst, send_sem=send, recv_sem=recv, device_id=to,
            device_id_type=MESH,
        )

    sib = dev(c=1 - c)
    ws = (wk, wv, wq)

    def cols(i):
        return pl.ds(pl.multiple_of(i * 256, 256), 256)

    def group(i):
        return pl.ds(pl.multiple_of(i * 128, 128), 128)

    slots = pl.ds(pl.multiple_of(y * 64 + c * 32, 32), 32)
    local = [
        pltpu.make_async_copy(tok, tokb.at[z, group(x)], loc.at[0]),
        pltpu.make_async_copy(sq.at[:, cols(x)], sqb, loc.at[1]),
        pltpu.make_async_copy(mem.at[slots, cols(x)], memb, loc.at[2]),
    ]
    last = [
        pltpu.make_async_copy(gain.at[:, cols(x)], gainb, loc.at[11]),
        pltpu.make_async_copy(dl, dlb, loc.at[12]),
    ]
    for m in range(3):
        local.append(
            pltpu.make_async_copy(ws[m].at[:, cols(x)], wb.at[m, y, x, c], loc.at[3 + m])
        )
    for cp in local + last:
        cp.start()

    barrier = pltpu.get_barrier_semaphore()

    def greet(p):
        pl.semaphore_signal(barrier, inc=1, device_id=p, device_id_type=MESH)

    greet(sib)
    for d in range(1, 4):
        greet(dev(x=xs[d]))
        greet(dev(y=ys[d]))
    pl.when(z < 3)(lambda: greet(dev(z=z + 1)))
    pl.when(z > 0)(lambda: greet(dev(z=z - 1)))
    pl.semaphore_wait(barrier, 9 - z // 3 - (3 - z) // 3)

    sent = []

    def go(cp):
        cp.start()
        sent.append(cp)

    first = 1 + z % 2
    third = 3 * (1 - z // 2)
    second = 6 - z - first - third
    order = [z, first, second, third]
    onward = [None, 3 * (z // 2), 3 - z, 3 * (z // 2)]
    middle = (z + 1) // 2 == 1

    def chain(i, src_of, send, recv):
        if i == 0:
            ref = src_of(z)
            up = remote(ref, ref, send.at[0], recv.at[z], dev(z=z + 1))
            down = remote(ref, ref, send.at[1], recv.at[z], dev(z=z - 1))
            return [(z < 3, up), (z > 0, down)]
        zi = order[i]
        ref = src_of(zi)
        return [(middle, remote(ref, ref, send.at[i + 1], recv.at[zi], dev(z=onward[i])))]

    def start_chain(*args):
        for cond, cp in chain(*args):
            pl.when(cond)(cp.start)

    def finish_chain(*args):
        for cond, cp in chain(*args):
            pl.when(cond)(cp.wait_send)

    def wait_chain(i, src_of, send, recv):
        ref = src_of(order[i])
        remote(ref, ref, send.at[0], recv.at[order[i]], sib).wait_recv()

    def half_rows(xi, h):
        return pl.ds(pl.multiple_of(xi * 128 + 64 * h, 64), 64)

    A = [(lambda zi, h=h: tokb.at[zi, half_rows(x, h)], z_s.at[h], z_r.at[h]) for h in (0, 1)]
    B = [(lambda zi, h=h: tokb.at[zi, half_rows(xs[2], h)], zb_s.at[h], zb_r.at[h]) for h in (0, 1)]

    def send_w(m):
        for d in (2, 1, 3):
            go(remote(ws[m].at[:, cols(xs[d])], wb.at[m, y, x, c], xw_s.at[m, d], xw_r.at[m, x],
                      dev(x=xs[d])))

    def send_x(i, h, k):
        zi = order[i]
        ref = tokb.at[zi, half_rows(x, h)]
        go(remote(ref, ref, xa_s.at[i, h, k], xa_r.at[zi, h, k], dev(x=xs[1 + 2 * k])))

    def wait_x(i, h, k):
        zi = order[i]
        ref = tokb.at[zi, half_rows(xs[3 - 2 * k], h)]
        remote(ref, ref, xa_s.at[0, 0, 0], xa_r.at[zi, h, k], sib).wait_recv()

    def wait_block(i):
        for h in (0, 1):
            for k in (0, 1):
                if i or h == k:
                    wait_x(i, h, k)

    def send_y(m, dx, src):
        for d in (2, 1, 3):
            go(remote(src, wb.at[m, y, xs[dx], c], yw_s.at[m, d, dx], yw_r.at[m, y, xs[dx]],
                      dev(y=ys[d])))

    def spread_own(m):
        send_y(m, 0, ws[m].at[:, cols(x)])

    def spread_w(m):
        for d in (1, 3, 2):
            ref = wb.at[m, y, xs[d], c]
            remote(ref, ref, xw_s.at[m, d], xw_r.at[m, xs[d]], sib).wait_recv()
            send_y(m, d, ref)
        local[3 + m].wait()
        ref = wb.at[m, y, :, c]
        go(remote(ref, ref, cw_s.at[m, 0], cw_r.at[m, y], sib))

    def pass_w(m):
        for d in (1, 3, 2):
            for dx in range(4):
                ref = wb.at[m, ys[d], xs[dx], c]
                remote(ref, ref, yw_s.at[m, d, dx], yw_r.at[m, ys[d], xs[dx]], sib).wait_recv()
            ref = wb.at[m, ys[d], :, c]
            go(remote(ref, ref, cw_s.at[m, d], cw_r.at[m, ys[d]], sib))

    def wait_w(m):
        for d in range(4):
            ref = wb.at[m, ys[d], :, 1 - c]
            remote(ref, ref, cw_s.at[m, d], cw_r.at[m, ys[d]], sib).wait_recv()

    def project(m, zi, fresh):
        w = wb[m, zi].reshape(1024, 256)
        r = jnp.dot(tokb[zi], w, preferred_element_type=F32)
        if fresh:
            acc[m] = r
        else:
            acc[m] += r

    def link(i, h, which):
        wait_chain(i, *which[h])
        start_chain(i, *which[h])

    def forward(h):
        ref = tokb.at[z, half_rows(xs[1 + 2 * h], h)]
        go(remote(ref, ref, f_s.at[h], f_r.at[h], dev(x=xs[3 - 2 * h])))

    def far(h):
        ref = tokb.at[z, half_rows(xs[2], h)]
        remote(ref, ref, f_s.at[h], f_r.at[h], sib).wait_recv()
        start_chain(0, *B[h])

    def pass_block(i):
        for h in (0, 1):
            link(i, h, A)
            send_x(i, h, 0)
            send_x(i, h, 1)

    def pass_far(i):
        for h in (0, 1):
            link(i, h, B)

    local[0].wait()
    start_chain(0, *A[0])
    send_x(0, 0, 1)
    send_x(0, 1, 0)
    spread_own(0)
    start_chain(0, *A[1])
    send_x(0, 1, 1)
    send_x(0, 0, 0)
    spread_own(1)
    wait_x(0, 0, 1)
    forward(0)
    wait_x(0, 1, 0)
    forward(1)
    send_w(0)
    pass_block(1)
    send_w(1)
    far(0)
    far(1)
    spread_w(0)
    pass_block(2)
    pass_far(1)
    spread_w(1)
    pass_block(3)
    send_w(2)
    spread_own(2)
    pass_w(0)
    pass_far(2)
    pass_w(1)
    pass_far(3)
    spread_w(2)
    wait_w(0)
    wait_w(1)
    for i, zi in enumerate(order):
        wait_block(i)
        project(0, zi, i == 0)
        project(1, zi, i == 0)

    local[1].wait()
    local[2].wait()
    for cp in last:
        cp.wait()
    length = dlb[0]
    j = lax.broadcasted_iota(jnp.int32, (1, 512), 1)
    valid = y * 1024 + (j // 128) * 256 + c * 128 + j % 128 < length
    stats = []
    for h in range(2):
        hc = slice(h * 128, (h + 1) * 128)
        k = acc[0, :, hc].astype(BF16)
        v = acc[1, :, hc].astype(BF16)
        s = lax.dot_general(sqb[:, hc], k, NT, preferred_element_type=F32) * SCALING
        s = jnp.where(valid, s, NEGATIVE)
        top = jnp.max(s, axis=1, keepdims=True)
        p = jnp.where(valid, jnp.exp(s - top), 0.0)
        total = jnp.sum(p, axis=1, keepdims=True)
        high = p.astype(BF16)
        low = (p - high.astype(F32)).astype(BF16)
        a = jnp.dot(high, v, preferred_element_type=F32) + jnp.dot(
            low, v, preferred_element_type=F32
        )
        for yy in range(4):
            for cc in range(2):
                r = yy * 64 + cc * 32
                pm[cc, yy, :, hc] = a[r : r + 32]
        stats.append((top, total))
    lanes = stat_lanes(stats, 256)
    for yy in range(4):
        for cc in range(2):
            r = yy * 64 + cc * 32
            pm[cc, yy, :, 256:384] = lanes[r : r + 32]

    cp = remote(pm.at[1 - c], pr, p1.at[0], p1.at[1], sib)
    go(cp)
    cp.wait_recv()
    outs, stats = merge([pm[c].reshape(128, 384), pr[...].reshape(128, 384)])
    mg[:, :, 0:128] = outs[0].reshape(4, 32, 128)
    mg[:, :, 128:256] = outs[1].reshape(4, 32, 128)
    mg[:, :, 256:384] = stat_lanes(stats, 128).reshape(4, 32, 128)
    for d in (2, 1, 3):
        go(remote(mg.at[ys[d]], mr.at[y], p2_s.at[d], p2_r.at[y], dev(y=ys[d])))

    for d in range(1, 4):
        remote(mr.at[ys[d]], mr.at[ys[d]], p2_s.at[d], p2_r.at[ys[d]], sib).wait_recv()
    outs, stats = merge([mg[y]] + [mr[ys[d]] for d in range(1, 4)])
    packed = jnp.concatenate([outs[h] / stats[h][1] for h in range(2)], axis=1)
    combined = memb[...].astype(F32) + packed
    stacked = jnp.concatenate([combined, combined * combined, jnp.zeros((64, 256), F32)], axis=0)
    sums = lax.dot_general(
        jnp.ones((8, 256), F32), stacked, NT, precision=lax.Precision.HIGHEST,
        preferred_element_type=F32,
    )
    st[x, z] = sums
    early = list(sent)
    sent.clear()
    for dz in (2, 3, 1, 0):
        for dx in (2, 1, 3, 0):
            if dx or dz:
                go(remote(st.at[x, z], st.at[x, z], p3_s.at[dx, dz], p3_r.at[x, z],
                          dev(x=xs[dx], z=zs[dz])))
    for dz in range(4):
        for dx in range(4):
            if dx or dz:
                ref = st.at[xs[dx], zs[dz]]
                remote(ref, ref, p3_s.at[dx, dz], p3_r.at[xs[dx], zs[dz]], sib).wait_recv()
    sums = jnp.sum(st[...].reshape(16, 8, 128), axis=0)
    column = jnp.transpose(sums)[:, 0:1] / D
    mean = column[0:32]
    square = column[32:64]
    inverse = lax.rsqrt(square - mean * mean + EPSILON)
    piece = ((combined - mean) * inverse * gainb[...]).astype(BF16)
    nmf[slots] = piece
    nx[:, cols(x)] = piece
    ref = nmf.at[slots]
    for d in (2, 1, 3):
        for cc in (0, 1):
            to = dev(y=ys[d], c=(c + cc) % 2)
            go(remote(ref, ref, p4_s.at[d, cc], p4_r.at[y, c], to))
    go(remote(ref, ref, p4_s.at[0, 1], p4_r.at[y, c], sib))
    for d in (2, 1, 3):
        go(remote(ref, nx.at[:, cols(x)], n_s.at[d], n_r.at[x], dev(x=xs[d])))

    pass_w(2)
    wait_w(2)
    for i in range(4):
        project(2, i, i == 0)
    for cp in early:
        cp.wait_send()
    for i in range(4):
        for h in (0, 1):
            finish_chain(i, *A[h])
            finish_chain(i, *B[h])

    for d in range(4):
        for cc in range(2):
            if d or cc:
                c2 = (c + cc) % 2
                ref = nmf.at[pl.ds(pl.multiple_of(ys[d] * 64 + c2 * 32, 32), 32)]
                remote(ref, ref, p4_s.at[d, cc], p4_r.at[ys[d], c2], sib).wait_recv()

    for d in range(1, 4):
        ref = nx.at[:, cols(xs[d])]
        remote(ref, ref, n_s.at[d], n_r.at[xs[d]], sib).wait_recv()
    final = [pltpu.make_async_copy(nx, o_nm.at[slots], loc.at[7])]
    final[0].start()
    for d in (2, 1, 3):
        go(remote(nx, o_nm.at[slots], m_s.at[d], m_r.at[y], dev(y=ys[d])))
    go(remote(nx, o_nm.at[slots], nc_s.at[0], nc_r.at[y], sib))

    r = lax.broadcasted_iota(jnp.int32, (128, 1), 0)
    for d in (2, 1, 3, 0):
        g = xs[d]
        live = y * 1024 + g * 256 + c * 128 + r < length
        for h in range(2):
            hc = slice(h * 128, (h + 1) * 128)
            q = acc[2, group(g), hc].astype(BF16)
            n = nmf[:, hc]
            s = lax.dot_general(q, n, NT, preferred_element_type=F32) * SCALING
            e = jnp.exp(s - jnp.max(s, axis=1, keepdims=True))
            probs = (e / jnp.sum(e, axis=1, keepdims=True)).astype(BF16)
            o = jnp.dot(probs, n, preferred_element_type=F32)
            ob[g, :, hc] = jnp.where(live, o, 0.0).astype(BF16)
        if d:
            go(remote(ob.at[g], o_un.at[:, cols(x)], u_s.at[d], u_r.at[x], dev(x=g)))
        else:
            cp = pltpu.make_async_copy(ob.at[g], o_un.at[:, cols(x)], loc.at[6])
            cp.start()
            final.append(cp)

    def rows_of(yi, ci):
        return o_nm.at[pl.ds(pl.multiple_of(yi * 64 + ci * 32, 32), 32)]

    for d in (1, 3, 2):
        ref = rows_of(ys[d], c)
        remote(ref, ref, m_s.at[d], m_r.at[ys[d]], sib).wait_recv()
        go(remote(ref, ref, nc_s.at[d], nc_r.at[ys[d]], sib))
    for d in range(1, 4):
        ref = o_un.at[:, cols(xs[d])]
        remote(ref, ref, u_s.at[d], u_r.at[xs[d]], sib).wait_recv()
    for d in range(4):
        ref = rows_of(ys[d], 1 - c)
        remote(ref, ref, nc_s.at[d], nc_r.at[ys[d]], sib).wait_recv()
    for cp in final:
        cp.wait()
    for cp in sent:
        cp.wait_send()


def on_device(tokens, w_key, w_value, w_query, slot_queries, memory, norm_gain, doc_length):
    dma = pltpu.SemaphoreType.DMA
    anywhere = pl.BlockSpec(memory_space=pltpu.HBM)
    return pl.pallas_call(
        kernel,
        out_shape=(
            pltpu.VMEM((128, 1024), BF16),
            pltpu.VMEM((256, 1024), BF16),
        ),
        in_specs=[anywhere] * 8,
        out_specs=(pl.BlockSpec(memory_space=pl.ANY),) * 2,
        scratch_shapes=[
            pltpu.VMEM((4, 512, 1024), BF16),
            pltpu.VMEM((3, 4, 4, 2, 128, 256), BF16),
            pltpu.VMEM((256, 256), BF16),
            pltpu.VMEM((32, 256), BF16),
            pltpu.VMEM((1, 256), F32),
            pltpu.SMEM((1,), jnp.int32),
            pltpu.VMEM((3, 512, 256), F32),
            pltpu.VMEM((2, 4, 32, 384), F32),
            pltpu.VMEM((4, 32, 384), F32),
            pltpu.VMEM((4, 32, 384), F32),
            pltpu.VMEM((4, 32, 384), F32),
            pltpu.VMEM((4, 4, 8, 128), F32),
            pltpu.VMEM((256, 256), BF16),
            pltpu.VMEM((32, 1024), BF16),
            pltpu.VMEM((4, 128, 256), BF16),
            dma((13,)),
            dma((2, 5)),
            dma((2, 4)),
            dma((2, 5)),
            dma((2, 4)),
            dma((4, 2, 2)),
            dma((4, 2, 2)),
            dma((2,)),
            dma((2,)),
            dma((3, 4)),
            dma((3, 4)),
            dma((3, 4, 4)),
            dma((3, 4, 4)),
            dma((3, 4)),
            dma((3, 4)),
            dma((2,)),
            dma((4,)),
            dma((4,)),
            dma((4, 4)),
            dma((4, 4)),
            dma((4, 2)),
            dma((4, 2)),
            dma((4,)),
            dma((4,)),
            dma((4,)),
            dma((4,)),
            dma((4,)),
            dma((4,)),
            dma((4,)),
            dma((4,)),
        ],
        compiler_params=pltpu.CompilerParams(
            collective_id=0, has_side_effects=True, vmem_limit_bytes=60 * 2**20
        ),
        name="luna",
    )(
        tokens, w_key, w_value, w_query, slot_queries, memory, norm_gain.reshape(1, 1024),
        doc_length,
    )


def solution(mesh):
    in_specs = (
        P(("dp", "seq"), "head"),
        P("seq", "head"),
        P("seq", "head"),
        P("seq", "head"),
        P("dp", "head"),
        P("dp", "head"),
        P("head"),
        P("dp"),
    )
    out_specs = (P(("dp", "seq"), "head"), P("dp", "head"))
    return jax.shard_map(
        on_device, mesh=mesh, in_specs=in_specs, out_specs=out_specs, check_vma=False
    )
```

profile of v0, /device:TPU:1, one launch (start us, length us, event | category | flops | bytes accessed | tf_op | source)
XLA Modules:
  0.0 77.5 jit_solution(5911710829453369134)
XLA Ops:
  1.3 74.7 %luna.1 = (bf16[128,1024]{1,0:T(8,128)(2,1)S(1)}, bf16[256,1024]{1,0:T(8,128)(2,1)S(1)}) custom-call(bf16[128,1024]{1,0:T(8,128)(2,1)} %tok.1, bf16[128,1024]{1,0:T(8,128)(2,1)} %wk.1, bf16[128,1024]{1,0:T(8,128)(2,1)} %wv.1, bf16[128,1024]{1,0:T(8,128)(2,1)} %wq.1, bf16[256,1024]{1,0:T(8,128)(2,1)} %sq.1, bf16[256,1024]{1,0:T(8,128)(2,1)} %mem.1, ...), custom_call_target="tpu_custom_call" | custom-call | tf_op jit(solution)/shard_map/luna/pallas_call | solution.py:419
  76.0 0.7 copy.12
  76.7 0.8 %copy.13 = bf16[256,1024]{1,0:T(8,128)(2,1)} copy(bf16[256,1024]{1,0:T(8,128)(2,1)S(1)} %get-tuple-element.3) | data formatting | bytes 1048576
where the time goes:
time: 77.6 us; the launch traced here: 77.5 us
  Pallas kernels  74.7 us (96%)
  local copies, waits for them, and re-layouts  1.5 us (2%)
  between operations  1.29 us (2%)
    pallas_call x1, Pallas kernels, on_device(): pl.pallas_call(kernel, out_shape=(pltpu.VMEM((128, 1024), BF16), pltpu.VM...  74.7 us

commit v1 on v0

--- a/solution.py
+++ b/solution.py
@@ -243,9 +243,9 @@
     send_w(0)
     pass_block(1)
     send_w(1)
+    spread_w(0)
     far(0)
     far(1)
-    spread_w(0)
     pass_block(2)
     pass_far(1)
     spread_w(1)
@@ -351,12 +351,6 @@
     wait_w(2)
     for i in range(4):
         project(2, i, i == 0)
-    for cp in early:
-        cp.wait_send()
-    for i in range(4):
-        for h in (0, 1):
-            finish_chain(i, *A[h])
-            finish_chain(i, *B[h])
 
     for d in range(4):
         for cc in range(2):
@@ -397,6 +391,12 @@
     def rows_of(yi, ci):
         return o_nm.at[pl.ds(pl.multiple_of(yi * 64 + ci * 32, 32), 32)]
 
+    for cp in early:
+        cp.wait_send()
+    for i in range(4):
+        for h in (0, 1):
+            finish_chain(i, *A[h])
+            finish_chain(i, *B[h])
     for d in (1, 3, 2):
         ref = rows_of(ys[d], c)
         remote(ref, ref, m_s.at[d], m_r.at[ys[d]], sib).wait_recv()
@@ -413,10 +413,21 @@
         cp.wait_send()
 
 
+def store(a, b, out_a, out_b, sem):
+    copies = [
+        pltpu.make_async_copy(a, out_a, sem.at[0]),
+        pltpu.make_async_copy(b, out_b, sem.at[1]),
+    ]
+    for cp in copies:
+        cp.start()
+    for cp in copies:
+        cp.wait()
+
+
 def on_device(tokens, w_key, w_value, w_query, slot_queries, memory, norm_gain, doc_length):
     dma = pltpu.SemaphoreType.DMA
     anywhere = pl.BlockSpec(memory_space=pltpu.HBM)
-    return pl.pallas_call(
+    results = pl.pallas_call(
         kernel,
         out_shape=(
             pltpu.VMEM((128, 1024), BF16),
@@ -479,6 +490,18 @@
         tokens, w_key, w_value, w_query, slot_queries, memory, norm_gain.reshape(1, 1024),
         doc_length,
     )
+    return pl.pallas_call(
+        store,
+        out_shape=(
+            jax.ShapeDtypeStruct((128, 1024), BF16),
+            jax.ShapeDtypeStruct((256, 1024), BF16),
+        ),
+        in_specs=[pl.BlockSpec(memory_space=pl.ANY)] * 2,
+        out_specs=(anywhere, anywhere),
+        scratch_shapes=[dma((2,))],
+        compiler_params=pltpu.CompilerParams(vmem_limit_bytes=2**20),
+        name="store",
+    )(*results)
 
 
 def solution(mesh):

time: 77.6 us -> 76.3 us (0.983)
  local copies, waits for them, and re-layouts: 1.5 us -> 0 us
    unnamed x2 -> x0, local copies, waits for them, and re-layouts: 1.5 us -> none
    pallas_call x0 -> x1, Pallas kernels: none -> 0.9 us  [on_device(): pl.pallas_call(store, out_shape=(jax.ShapeDtypeStruct((128, 1024), BF16),...]
where the time goes in v1:
time: 76.3 us; the launch traced here: 76.2 us
  Pallas kernels  75 us (98%)
  between operations  1.29 us (2%)
    pallas_call x1, Pallas kernels, on_device(): pl.pallas_call(kernel, out_shape=(pltpu.VMEM((128, 1024), BF16), pltpu.VM...  74.1 us

profile of v1, /device:TPU:1, one launch (start us, length us, event | category | flops | bytes accessed | tf_op | source)
XLA Modules:
  0.0 76.2 jit_solution(347540464888074034)
XLA Ops:
  1.3 74.1 %luna.1 = (bf16[128,1024]{1,0:T(8,128)(2,1)S(1)}, bf16[256,1024]{1,0:T(8,128)(2,1)S(1)}) custom-call(bf16[128,1024]{1,0:T(8,128)(2,1)} %tok.1, bf16[128,1024]{1,0:T(8,128)(2,1)} %wk.1, bf16[128,1024]{1,0:T(8,128)(2,1)} %wv.1, bf16[128,1024]{1,0:T(8,128)(2,1)} %wq.1, bf16[256,1024]{1,0:T(8,128)(2,1)} %sq.1, bf16[256,1024]{1,0:T(8,128)(2,1)} %mem.1, ...), custom_call_target="tpu_custom_call" | custom-call | tf_op jit(solution)/shard_map/luna/pallas_call | solution.py:430
  75.3 0.9 %store.1 = (bf16[128,1024]{1,0:T(8,128)(2,1)}, bf16[256,1024]{1,0:T(8,128)(2,1)}) custom-call(bf16[128,1024]{1,0:T(8,128)(2,1)S(1)} %get-tuple-element.4.a, bf16[256,1024]{1,0:T(8,128)(2,1)S(1)} %get-tuple-element.5.b), custom_call_target="tpu_custom_call" | custom-call | tf_op jit(solution)/shard_map/store/pallas_call | solution.py:493

commit v2 on v1

--- a/solution.py
+++ b/solution.py
@@ -258,11 +258,19 @@
     pass_far(3)
     spread_w(2)
     wait_w(0)
+    for i in (0, 1):
+        wait_block(i)
+        project(0, order[i], i == 0)
+    for i in (2,):
+        wait_block(i)
+        project(0, order[i], i == 0)
     wait_w(1)
-    for i, zi in enumerate(order):
+    for i in (0, 1, 2):
+        project(1, order[i], i == 0)
+    for i in (3,):
         wait_block(i)
-        project(0, zi, i == 0)
-        project(1, zi, i == 0)
+        project(0, order[i], i == 0)
+        project(1, order[i], i == 0)
 
     local[1].wait()
     local[2].wait()
@@ -325,6 +333,7 @@
             if dx or dz:
                 go(remote(st.at[x, z], st.at[x, z], p3_s.at[dx, dz], p3_r.at[x, z],
                           dev(x=xs[dx], z=zs[dz])))
+    pass_w(2)
     for dz in range(4):
         for dx in range(4):
             if dx or dz:
@@ -347,7 +356,6 @@
     for d in (2, 1, 3):
         go(remote(ref, nx.at[:, cols(x)], n_s.at[d], n_r.at[x], dev(x=xs[d])))
 
-    pass_w(2)
     wait_w(2)
     for i in range(4):
         project(2, i, i == 0)

time: 76.3 us -> 76 us (level)
  no operation moved by 1% of the time
where the time goes in v2:
time: 76 us; the launch traced here: 75.9 us
  Pallas kernels  74.7 us (98%)
  between operations  1.29 us (2%)
    pallas_call x1, Pallas kernels, on_device(): pl.pallas_call(kernel, out_shape=(pltpu.VMEM((128, 1024), BF16), pltpu.VM...  73.8 us

profile of v2, /device:TPU:1, one launch (start us, length us, event | category | flops | bytes accessed | tf_op | source)
XLA Modules:
  0.0 75.9 jit_solution(3825339477782246667)
XLA Ops:
  1.3 73.8 %luna.1 = (bf16[128,1024]{1,0:T(8,128)(2,1)S(1)}, bf16[256,1024]{1,0:T(8,128)(2,1)S(1)}) custom-call(bf16[128,1024]{1,0:T(8,128)(2,1)} %tok.1, bf16[128,1024]{1,0:T(8,128)(2,1)} %wk.1, bf16[128,1024]{1,0:T(8,128)(2,1)} %wv.1, bf16[128,1024]{1,0:T(8,128)(2,1)} %wq.1, bf16[256,1024]{1,0:T(8,128)(2,1)} %sq.1, bf16[256,1024]{1,0:T(8,128)(2,1)} %mem.1, ...), custom_call_target="tpu_custom_call" | custom-call | tf_op jit(solution)/shard_map/luna/pallas_call | solution.py:438
  75.0 0.9 %store.1 = (bf16[128,1024]{1,0:T(8,128)(2,1)}, bf16[256,1024]{1,0:T(8,128)(2,1)}) custom-call(bf16[128,1024]{1,0:T(8,128)(2,1)S(1)} %get-tuple-element.4.a, bf16[256,1024]{1,0:T(8,128)(2,1)S(1)} %get-tuple-element.5.b), custom_call_target="tpu_custom_call" | custom-call | tf_op jit(solution)/shard_map/store/pallas_call | solution.py:501

commit v3 on v2

--- a/solution.py
+++ b/solution.py
@@ -240,6 +240,7 @@
     forward(0)
     wait_x(0, 1, 0)
     forward(1)
+    spread_own(2)
     send_w(0)
     pass_block(1)
     send_w(1)
@@ -251,7 +252,6 @@
     spread_w(1)
     pass_block(3)
     send_w(2)
-    spread_own(2)
     pass_w(0)
     pass_far(2)
     pass_w(1)

time: 76 us -> 75.6 us (level)
  no operation moved by 1% of the time
where the time goes in v3:
time: 75.6 us; the launch traced here: 75.5 us
  Pallas kernels  74.2 us (98%)
  between operations  1.29 us (2%)
    pallas_call x1, Pallas kernels, on_device(): pl.pallas_call(kernel, out_shape=(pltpu.VMEM((128, 1024), BF16), pltpu.VM...  73.3 us

profile of v3, /device:TPU:1, one launch (start us, length us, event | category | flops | bytes accessed | tf_op | source)
XLA Modules:
  0.0 75.5 jit_solution(15695991058163047172)
XLA Ops:
  1.3 73.3 %luna.1 = (bf16[128,1024]{1,0:T(8,128)(2,1)S(1)}, bf16[256,1024]{1,0:T(8,128)(2,1)S(1)}) custom-call(bf16[128,1024]{1,0:T(8,128)(2,1)} %tok.1, bf16[128,1024]{1,0:T(8,128)(2,1)} %wk.1, bf16[128,1024]{1,0:T(8,128)(2,1)} %wv.1, bf16[128,1024]{1,0:T(8,128)(2,1)} %wq.1, bf16[256,1024]{1,0:T(8,128)(2,1)} %sq.1, bf16[256,1024]{1,0:T(8,128)(2,1)} %mem.1, ...), custom_call_target="tpu_custom_call" | custom-call | tf_op jit(solution)/shard_map/luna/pallas_call | solution.py:438
  74.6 0.9 %store.1 = (bf16[128,1024]{1,0:T(8,128)(2,1)}, bf16[256,1024]{1,0:T(8,128)(2,1)}) custom-call(bf16[128,1024]{1,0:T(8,128)(2,1)S(1)} %get-tuple-element.4.a, bf16[256,1024]{1,0:T(8,128)(2,1)S(1)} %get-tuple-element.5.b), custom_call_target="tpu_custom_call" | custom-call | tf_op jit(solution)/shard_map/store/pallas_call | solution.py:501
